TPU v7x, 1024 devices: a whole 4x8x16 slice. The times are simulated.
1024 devices in a mesh: sub: 128 (over z, y_lo, core), grp: 4 (over x), rep: 2 (over y_hi).
Axes of the slice: x: 4, y: 8 (y_hi: 2, y_lo: 4; y = y_hi * 4 + y_lo), z: 16, core: 2. Of those that a mesh axis runs over, the one named last changes fastest.
Arguments:
- residual: float32 [524288, 128], P(('sub', 'grp', 'rep'))
- direction: float32 [524288, 128], P(('sub', 'grp', 'rep'))
- sub_blocks: bfloat16 [16384, 4, 128, 128], P(('sub', 'grp', 'rep')), may hold values from -0.15625 to 0.15625
- pattern: int32 [16384, 4], P(('sub', 'grp', 'rep')), may hold values from 0 to 15
- facing_block_lookup: int32 [1024, 4], P(('sub', 'grp', 'rep')), may hold values from 0 to 3, each once within a row
- corners: int32 [1024, 8], P(('sub', 'grp', 'rep')), may hold values from 0 to 511, as said below
- coarse_inverse: float32 [8192, 8192], P(('sub', 'grp', 'rep')), as said below
Outputs:
- residual_new: float32 [524288, 128], P(('sub', 'grp', 'rep'))
- direction_new: float32 [524288, 128], P(('sub', 'grp', 'rep'))
Inputs may be any that keep to these rules, and one draw needn't show every extreme that they name: `pattern`: block indices of the subdomain's own node blocks, repeats allowed. `facing_block_lookup`: each row is a permutation. `corners`: entry i of a row lies in i * 64 to (i + 1) * 64 - 1. `coarse_inverse`: symmetric.
All inputs are finite; a program needn't handle non-finite values.
Results may differ from a plain program's by a relative error of at most 0.002.
Values sent between devices are 32-bit elements; how exact they have to be, the bound alone decides.
A program may use at most 32 MiB of HBM per device.

v0:
```python
import jax
import jax.numpy as jnp
from jax import lax
from jax.sharding import PartitionSpec as P

SWEEPS = 3


def shifted(array, axis, by):
    length = lax.axis_size(axis)
    pairs = [(i, i + by) for i in range(length) if 0 <= i + by < length]
    return lax.ppermute(array, axis, pairs)


def relax(sub_blocks, pattern, source):
    relaxed = source
    for sweep_index in range(SWEEPS):
        rounded = relaxed.astype(jnp.bfloat16)
        picked = rounded[pattern]
        product = jnp.einsum(
            "rkij,rkjt->rit", sub_blocks, picked, preferred_element_type=jnp.float32
        )
        relaxed = source - product
    return relaxed


def per_device(
    residual, direction, sub_blocks, pattern, facing_block_lookup, corners, coarse_inverse
):
    face_rows, tracks = residual.shape
    face_blocks = facing_block_lookup.shape[1]
    block_size = sub_blocks.shape[2]
    row_blocks = sub_blocks.shape[0]
    norm_old = lax.psum(jnp.sum(residual * residual, axis=0), ("sub", "grp", "rep"))
    block_chooser = (
        facing_block_lookup[0][:, None] == jnp.arange(face_blocks, dtype=jnp.int32)[None, :]
    ).astype(jnp.float32)
    local_subdomain_blocks = direction.reshape(face_blocks, block_size, tracks)
    sent_interface_blocks = jnp.einsum(
        "vi,iso->vso", block_chooser, local_subdomain_blocks, precision=lax.Precision.HIGHEST
    )
    incoming = shifted(sent_interface_blocks.reshape(face_rows, tracks), ("sub", "grp", "rep"), 1)
    interior = jnp.zeros(((row_blocks - 2 * face_blocks) * block_size, tracks), jnp.float32)
    source = jnp.concatenate([-incoming, direction, interior], axis=0).reshape(
        row_blocks, block_size, tracks
    )
    relaxed = relax(sub_blocks, pattern, source)
    upper = relaxed[face_blocks : 2 * face_blocks].reshape(face_rows, tracks)
    lower = relaxed[:face_blocks].reshape(face_rows, tracks)
    arrived = shifted(lower, ("sub", "grp", "rep"), -1)
    mapped = jnp.einsum(
        "mw,mpf->wpf",
        block_chooser,
        arrived.reshape(face_blocks, block_size, tracks),
        precision=lax.Precision.HIGHEST,
    ).reshape(face_rows, tracks)
    summed = upper + mapped
    jumped = upper - mapped
    picker = (corners[0][:, None] == jnp.arange(face_rows, dtype=jnp.int32)[None, :]).astype(
        jnp.float32
    )
    corner_totals = jnp.dot(
        picker, summed, precision=lax.Precision.HIGHEST, preferred_element_type=jnp.float32
    )
    coarse_part = jnp.dot(
        coarse_inverse,
        lax.all_gather(corner_totals, ("sub", "grp", "rep"), axis=0, tiled=True),
        precision=lax.Precision.HIGHEST,
        preferred_element_type=jnp.float32,
    )
    image = jumped + jnp.dot(
        picker.T, coarse_part, precision=lax.Precision.HIGHEST, preferred_element_type=jnp.float32
    )
    local_cross = jnp.sum(residual * image, axis=0)
    local_curve = jnp.sum(image * image, axis=0)
    cross, curvature = lax.psum((local_cross, local_curve), ("sub", "grp", "rep"))
    step_length = cross / curvature
    residual_new = residual - step_length * image
    norm_new = lax.psum(jnp.sum(residual_new * residual_new, axis=0), ("sub", "grp", "rep"))
    direction_new = residual_new + norm_new / norm_old * direction
    return (residual_new, direction_new)


def solution(mesh):
    in_specs = (
        P(("sub", "grp", "rep"), None),
        P(("sub", "grp", "rep"), None),
        P(("sub", "grp", "rep"), None, None, None),
        P(("sub", "grp", "rep"), None),
        P(("sub", "grp", "rep"), None),
        P(("sub", "grp", "rep"), None),
        P(("sub", "grp", "rep"), None),
    )
    out_specs = (P(("sub", "grp", "rep"), None), P(("sub", "grp", "rep"), None))
    return jax.shard_map(
        per_device, mesh=mesh, in_specs=in_specs, out_specs=out_specs, check_vma=False
    )
```

profile of v0, /device:TPU:1, one launch (start us, length us, event | category | flops | bytes accessed | tf_op | source)
XLA Modules:
  0.0 2432.2 jit_solution(1946235642235932123)
XLA Ops:
  7.2 1.7 fusion.7
  8.9 8.3 collective-permute-start
  17.2 0.7 compare_select_fusion
  18.1 7.7 collective-permute-done
  25.8 1.3 maximum_maximum_fusion
  27.1 0.9 convert_element_type.11
  28.0 1.3 copy.22
  29.3 3.2 gather_fusion
  32.5 3.4 fusion.4
  36.0 3.2 gather_fusion.1
  39.2 3.4 fusion.3
  42.5 3.2 gather_fusion.2
  45.7 2.3 fusion.2
  48.1 11.7 collective-permute-start.1
  59.8 7.2 collective-permute-done.1
  67.0 0.5 fusion.5
  67.6 0.8 fusion.10
  68.4 2109.2 %all-gather.2.cloned.1.call-done = f32[8192,128]{1,0:T(8,128)} async-done(((f32[8,128]{1,0:T(8,128)}), f32[8192,128]{1,0:T(8,128)}) %all-gather.2.cloned.1.call-update) | async-done | bytes 4194320 | tf_op jit(solution)/shard_map/all_gather | solution.py:67
  2177.7 8.5 fusion.19
  2186.2 0.4 multiply_reduce_fusion
  2186.6 119.0 %all-reduce.1 = (f32[128]{0:T(128)S(1)}, f32[128]{0:T(128)S(1)}) all-reduce(f32[128]{0:T(128)S(1)} %get-tuple-element.3, f32[128]{0:T(128)S(1)} %get-tuple-element.4), channel_id=1, replica_groups=mesh['sub'=128,'grp'=4,'rep'=2] {'sub','grp','rep'}, use_global_device_ids=true, to_apply=%region_1.0 | all-reduce | flops 256 | bytes 2048 | tf_op jit(solution)/shard_map/psum | solution.py:76
  2305.6 0.1 multiply_reduce_fusion.1
  2305.7 119.0 %all-reduce = (f32[128]{0:T(128)S(1)}, f32[128]{0:T(128)S(1)}) all-reduce(f32[128]{0:T(128)S(1)} %get-tuple-element.9, f32[128]{0:T(128)S(1)} %get-tuple-element.2), channel_id=1, replica_groups=mesh['sub'=128,'grp'=4,'rep'=2] {'sub','grp','rep'}, use_global_device_ids=true, to_apply=%region_5.0 | all-reduce | flops 256 | bytes 2048 | tf_op jit(solution)/shard_map/psum | solution.py:79
  2424.6 0.7 multiply_add_fusion
  (27 shorter events, 0.4 us)
Async XLA Ops:
  7.2 25.4 %copy-start = (bf16[16,4,128,128]{3,2,1,0:T(8,128)(2,1)S(1)}, bf16[16,4,128,128]{3,2,1,0:T(8,128)(2,1)}, u32[]{:S(2)}) copy-start(bf16[16,4,128,128]{3,2,1,0:T(8,128)(2,1)} %param.9) | copy-start | bytes 6291460
  7.2 2170.5 %all-gather.2.cloned.1.call-start = ((), (), s32[]{:S(2)}) async-start(), calls=%async_computation | async-start | bytes 4198400 | tf_op jit(solution)/shard_map/all_gather | solution.py:67
  8.9 16.9 collective-permute-start
  45.7 21.3 copy-start.5
  48.0 19.5 copy-start.6
  48.1 2129.6 %copy-start.4 = (f32[8,8192]{1,0:T(8,128)S(1)}, f32[8,8192]{1,0:T(8,128)}, u32[]{:S(2)}) copy-start(f32[8,8192]{1,0:T(8,128)} %param.13) | copy-start | bytes 786436
  48.1 18.9 collective-permute-start.1
  68.4 2117.7 %copy-start.2 = (f32[512,128]{1,0:T(8,128)S(1)}, f32[512,128]{1,0:T(8,128)}, u32[]{:S(2)}) copy-start(f32[512,128]{1,0:T(8,128)} %param.7) | copy-start | bytes 786436
  68.4 2356.2 %copy-start.1 = (f32[512,128]{1,0:T(8,128)S(1)}, f32[512,128]{1,0:T(8,128)}, u32[]{:S(2)}) copy-start(f32[512,128]{1,0:T(8,128)} %param.8) | copy-start | bytes 786436
  2305.7 119.7 %copy-start.3 = (f32[512,128]{1,0:T(8,128)}, f32[512,128]{1,0:T(8,128)S(1)}, u32[]{:S(2)}) copy-start(f32[512,128]{1,0:T(8,128)S(1)} %get-tuple-element.10) | copy-start | bytes 786436
Sparse Core Ops, SparseCore 0:
  68.5 2109.1 all-gather.1
where the time goes:
time: 2430 us
  waiting for transfers between devices  2120 us (87%)
  blocking collectives  238 us (10%)
    all_gather x1, waiting for transfers between devices, per_device(): lax.all_gather(corner_totals, ('sub', 'grp', 'rep'), axis=0, tiled=True)  2110 us
    psum x1, blocking collectives, per_device(): lax.psum((local_cross, local_curve), ('sub', 'grp', 'rep'))  119 us
    psum x1, blocking collectives, per_device(): lax.psum(jnp.sum(residual_new * residual_new, axis=0), ('sub', 'grp', 're...  119 us
  transfers between devices with their start and end apart: 3, of which 3 were waited for; matrix products, arithmetic and copies ran while one was open for 0% of the time, Pallas kernels for 0%

commit v1 on v0

v1 whole, which is shorter than its diff:
```python
import functools

import jax
import jax.numpy as jnp
from jax import lax
from jax.experimental import pallas as pl
from jax.experimental.pallas import tpu as pltpu
from jax.sharding import PartitionSpec as P

MESH = pl.DeviceIdType.MESH
AXES = ("sub", "grp", "rep")
SWEEPS = 3
CORES = 2
LANES = 128


def two_sum(a, b):
    s = a + b
    t = s - a
    return s, (a - (s - t)) + (b - t)


def split(a):
    c = a * 4097.0
    hi = c - (c - a)
    return hi, a - hi


def two_product(a, b):
    p = a * b
    ah, al = split(a)
    bh, bl = split(b)
    return p, ((ah * bh - p) + ah * bl + al * bh) + al * bl


def pair_add(a, b):
    s, e = two_sum(a[0], b[0])
    return s, e + (a[1] + b[1])


def tidy(a):
    s = a[0] + a[1]
    return s, a[1] - (s - a[0])


def add_product(total, a, b):
    p, e = two_product(a, b)
    return pair_add(total, (p, e))


def fold(pair, axis=0):
    while pair[0].shape[axis] > 1:
        half = pair[0].shape[axis] // 2
        pair = pair_add(
            tuple(lax.slice_in_dim(v, 0, half, axis=axis) for v in pair),
            tuple(lax.slice_in_dim(v, half, 2 * half, axis=axis) for v in pair),
        )
    return pair


def kernel(
    sizes,
    pattern,
    facing,
    corners,
    residual_hbm,
    direction_hbm,
    blocks_hbm,
    coarse_hbm,
    image,
    factors,
    residual,
    direction,
    blocks,
    coarse,
    source,
    rounded,
    upper,
    forward_out,
    forward_in,
    back_out,
    back_in,
    corner_out,
    corner_in,
    packed,
    columns,
    turned,
    totals,
    part,
    part_in,
    sums_plane,
    sums_line,
    load_sem,
    forward_send,
    forward_recv,
    back_send,
    back_recv,
    corner_send,
    corner_recv,
    group_send,
    group_recv,
):
    n_z, n_yl, n_grp, n_rep = sizes
    n_line, n_plane = n_z * CORES, n_yl * n_grp * n_rep
    count = n_line * n_plane
    faces, block, tracks = forward_in.shape[0], direction.shape[1], direction.shape[2]
    row_blocks, nnz = blocks.shape[:2]
    n_corners = corners.shape[1]
    segment = faces * block // n_corners
    per_block = block // segment

    sub, grp, rep = (lax.axis_index(a) for a in AXES)
    k = (sub * n_grp + grp) * n_rep + rep
    core, yl, z = sub % CORES, (sub // CORES) % n_yl, sub // (CORES * n_yl)
    line = z * CORES + core
    plane = (yl * n_grp + grp) * n_rep + rep

    def device_of(index):
        return (index // (n_grp * n_rep), (index // n_rep) % n_grp, index % n_rep)

    def on_line(place):
        return ((place // CORES * n_yl + yl) * CORES + place % CORES, grp, rep)

    def on_plane(place):
        there = (z * n_yl + place // (n_grp * n_rep)) * CORES + core
        return (there, (place // n_rep) % n_grp, place % n_rep)

    above, below = device_of((k + 1) % count), device_of((k + count - 1) % count)

    barrier = pltpu.get_barrier_semaphore()

    def greet(device):
        pl.semaphore_signal(barrier, inc=1, device_id=device, device_id_type=MESH)

    greet(above)
    greet(below)

    @pl.loop(1, n_line)
    def _(j):
        greet(on_line((line + j) % n_line))

    @pl.loop(1, n_plane)
    def _(j):
        greet(on_plane((plane + j) % n_plane))

    loads = [
        pltpu.make_async_copy(a, b, load_sem.at[i])
        for i, (a, b) in enumerate(
            ((direction_hbm, direction), (coarse_hbm, coarse), (residual_hbm, residual), (blocks_hbm, blocks))
        )
    ]
    for load in loads:
        load.start()

    back_at = []
    for v in range(faces):
        place = jnp.int32(0)
        for b in range(faces):
            place = jnp.where(facing[0, b] == v, b, place)
        back_at.append(place)

    loads[0].wait()
    for b in range(faces):
        forward_out[b, :block] = direction[facing[0, b]]
    rows8 = lax.broadcasted_iota(jnp.int32, (n_corners, tracks), 0)
    wanted = jnp.zeros((n_corners, tracks), jnp.int32)
    for i in range(n_corners):
        wanted = jnp.where(rows8 == i, back_at[i // per_block] * block + corners[0, i] % block, wanted)
    forward_out[faces - 1, block:] = wanted.astype(jnp.float32)

    loads[1].wait()
    lanes = lax.broadcasted_iota(jnp.int32, (n_corners, LANES), 1)
    half = LANES // CORES
    for zz in range(n_z):
        for q in range(n_yl // CORES):
            first = coarse[:, pl.ds((zz * n_yl + 2 * q) * LANES, LANES)]
            second = coarse[:, pl.ds((zz * n_yl + 2 * q + 1) * LANES, LANES)]
            at = pl.ds(q * LANES, LANES)
            packed[zz * CORES, :, at] = jnp.where(lanes < half, first, pltpu.roll(second, half, 1))
            packed[zz * CORES + 1, :, at] = jnp.where(lanes < half, pltpu.roll(first, half, 1), second)

    pl.semaphore_wait(barrier, n_line + n_plane)

    def remote(source_ref, target_ref, send, recv, device):
        return pltpu.make_async_remote_copy(
            src_ref=source_ref,
            dst_ref=target_ref,
            send_sem=send,
            recv_sem=recv,
            device_id=device,
            device_id_type=MESH,
        )

    forward = []
    for b in range(faces):
        rows = pl.ds(0, block if b < faces - 1 else block + n_corners)
        forward.append(
            remote(forward_out.at[b, rows], forward_in.at[b, rows], forward_send.at[b], forward_recv.at[b], above)
        )
        forward[-1].start()

    def exchange(stage, size, mine, where, source_of, target):
        @pl.loop(1, size)
        def _(j):
            there = (mine + j) % size
            remote(
                source_of(there), target.at[mine], group_send.at[stage], group_recv.at[stage], where(there)
            ).start()

    def all_of(stage, size, target, sems):
        rest = target.at[pl.ds(0, size - 1)]
        return pltpu.make_async_copy(rest, rest, sems.at[stage])

    exchange(0, n_line, line, on_line, lambda there: packed.at[there], columns)
    columns[line] = packed[line]

    rows32 = 32
    zero = (jnp.zeros((rows32, tracks), jnp.float32),) * 2
    loads[2].wait()

    def add_old(i, total):
        r = residual[pl.ds(pl.multiple_of(i * rows32, rows32), rows32)]
        return add_product(total, r, r)

    old = fold(lax.fori_loop(0, faces * block // rows32, add_old, zero))
    for r in range(2 * faces, row_blocks):
        source[r] = jnp.zeros((block, tracks), jnp.float32)
        rounded[0, r] = jnp.zeros((block, tracks), rounded.dtype)
    for b in range(faces):
        source[faces + b] = direction[b]
        rounded[0, faces + b] = direction[b].astype(rounded.dtype)
    loads[3].wait()
    for b in range(faces):
        forward[b].wait_recv()
    for b in range(faces):
        arrived = jnp.where(k > 0, -forward_in[b, :block], 0.0)
        source[b] = arrived
        rounded[0, b] = arrived.astype(rounded.dtype)

    def relaxed(r, now):
        left = jnp.concatenate([blocks[r, j] for j in range(nnz)], axis=1)
        right = jnp.concatenate([rounded[now, pattern[r, j]] for j in range(nnz)], axis=0)
        return source[r] - jnp.dot(left, right, preferred_element_type=jnp.float32)

    for sweep in range(SWEEPS - 1):

        def step(r, carry, now=sweep % 2):
            rounded[1 - now, r] = relaxed(r, now).astype(rounded.dtype)
            return carry

        lax.fori_loop(0, row_blocks, step, 0, unroll=4)
    last = (SWEEPS - 1) % 2

    def step_lower(r, carry):
        back_out[r] = relaxed(r, last)
        return carry

    lax.fori_loop(0, faces, step_lower, 0, unroll=True)

    rows_seg = lax.broadcasted_iota(jnp.int32, (segment, tracks), 0)
    found = jnp.zeros((n_corners, tracks), jnp.float32)
    for i in range(n_corners):
        at = forward_in[faces - 1, block + i : block + i + 1].astype(jnp.int32)
        low = (i % per_block) * segment
        sought = jnp.zeros((8, tracks), jnp.float32)
        for b in range(faces):
            piece = back_out[b, low : low + segment]
            hit = jnp.where(rows_seg + (b * block + low) == at, piece, 0.0)
            sought = sought + jnp.sum(hit.reshape(segment // 8, 8, tracks), axis=0)
        found = jnp.where(rows8 == i, jnp.sum(sought, axis=0, keepdims=True), found)
    corner_out[...] = found
    corner_copy = remote(corner_out, corner_in, corner_send, corner_recv, below)
    corner_copy.start()
    back = [
        remote(back_out.at[b], back_in.at[b], back_send.at[b], back_recv.at[b], below) for b in range(faces)
    ]
    for copy in back:
        copy.start()

    def step_upper(r, carry):
        upper[pl.ds(pl.multiple_of((r - faces) * block, block), block)] = relaxed(r, last)
        return carry

    lax.fori_loop(faces, 2 * faces, step_upper, 0, unroll=True)
    own = jnp.zeros((n_corners, tracks), jnp.float32)
    for i in range(n_corners):
        own = jnp.where(rows8 == i, upper[pl.ds(corners[0, i], 1)], own)

    all_of(0, n_line, columns, group_recv).wait()
    turned[...] = columns[...].reshape(n_line * n_corners, n_plane * n_corners).T

    corner_copy.wait_recv()
    at_corners = jnp.where(k < count - 1, corner_in[...], 0.0)
    totals[line] = own + at_corners
    exchange(1, n_line, line, on_line, lambda there: totals.at[line], totals)
    own_jump = own - at_corners
    own_residual = jnp.zeros((n_corners, tracks), jnp.float32)
    for i in range(n_corners):
        own_residual = jnp.where(rows8 == i, residual[pl.ds(corners[0, i], 1)], own_residual)

    all_of(1, n_line, totals, group_recv).wait()
    part[...] = jnp.dot(
        turned[...],
        totals[...].reshape(n_line * n_corners, tracks),
        precision=lax.Precision.HIGHEST,
        preferred_element_type=jnp.float32,
    ).reshape(n_plane, n_corners, tracks)
    exchange(2, n_plane, plane, on_plane, lambda there: part.at[there], part_in)
    part_in[plane] = part[plane]

    for copy in back:
        copy.wait_recv()
    rows_in = lax.broadcasted_iota(jnp.int32, (rows32, tracks), 0)
    cross, curve = zero, zero
    for i in range(n_corners):
        for piece in range(segment // rows32):
            start = i * segment + piece * rows32
            v, low = start // block, start % block
            mapped = jnp.where(k < count - 1, back_in[back_at[v], low : low + rows32], 0.0)
            jump = upper[start : start + rows32] - mapped
            image[start : start + rows32] = jump
            jump = jnp.where(rows_in + start == corners[0, i], 0.0, jump)
            cross = add_product(cross, residual[start : start + rows32], jump)
            curve = add_product(curve, jump, jump)
    cross = fold((cross[0].reshape(4, 8, tracks), cross[1].reshape(4, 8, tracks)))
    curve = fold((curve[0].reshape(4, 8, tracks), curve[1].reshape(4, 8, tracks)))

    all_of(2, n_plane, part_in, group_recv).wait()
    coarse_part = jnp.sum(part_in[...], axis=0)
    at_nodes = own_jump + coarse_part
    cross = fold(tuple(v.reshape(n_corners, tracks) for v in add_product(cross, own_residual, at_nodes)))
    curve = fold(tuple(v.reshape(n_corners, tracks) for v in add_product(curve, at_nodes, at_nodes)))

    mine = jnp.concatenate([old[0], cross[0], curve[0], old[1], cross[1], curve[1]], axis=1)
    sums_plane[plane] = mine
    exchange(3, n_plane, plane, on_plane, lambda there: sums_plane.at[plane], sums_plane)
    for i in range(n_corners):
        for piece in range(segment // rows32):
            start = i * segment + piece * rows32
            added = jnp.where(rows_in + start == corners[0, i], coarse_part[i : i + 1], 0.0)
            image[start : start + rows32] = image[start : start + rows32] + added

    def total_of(buffer):
        pair = fold((buffer[:, :, : 3 * tracks], buffer[:, :, 3 * tracks :]))
        return tuple(v.reshape(1, 3 * tracks) for v in tidy(pair))

    all_of(3, n_plane, sums_plane, group_recv).wait()
    sums_line[line] = jnp.concatenate(total_of(sums_plane), axis=1)
    exchange(4, n_line, line, on_line, lambda there: sums_line.at[line], sums_line)
    all_of(4, n_line, sums_line, group_recv).wait()
    pair = total_of(sums_line)
    old, cross, curve = (
        tuple(v[:, i * tracks : (i + 1) * tracks] for v in pair) for i in range(3)
    )
    length = cross[0] / curve[0]
    scale = 2.0**-14
    old, cross, curve = (tuple(v * scale for v in pair) for pair in (old, cross, curve))
    inner, inner_low = two_product(-length, curve[0])
    inner = tidy(pair_add((2.0 * cross[0], 2.0 * cross[1]), (inner, inner_low - length * curve[1])))
    outer, outer_low = two_product(-length, inner[0])
    new = tidy(pair_add(old, (outer, outer_low - length * inner[1])))
    factors[0:1] = length
    factors[1:2] = jnp.maximum(new[0], 0.0) / old[0]

    for copy in forward + back:
        copy.wait_send()
    corner_copy.wait_send()
    for stage, (size, buffer) in enumerate(
        ((n_line, columns), (n_line, totals), (n_plane, part_in), (n_plane, sums_plane), (n_line, sums_line))
    ):
        all_of(stage, size, buffer, group_send).wait()


def per_device(sizes, residual, direction, sub_blocks, pattern, facing, corners, coarse_inverse):
    n_z, n_yl, n_grp, n_rep = sizes
    n_line, n_plane = n_z * CORES, n_yl * n_grp * n_rep
    face_rows, tracks = residual.shape
    row_blocks, nnz, block, _ = sub_blocks.shape
    faces, n_corners = facing.shape[1], corners.shape[1]
    f32, vmem = jnp.float32, pltpu.VMEM
    dma = pltpu.SemaphoreType.DMA
    image, factors = pl.pallas_call(
        functools.partial(kernel, sizes),
        out_shape=(jax.ShapeDtypeStruct((face_rows, tracks), f32), jax.ShapeDtypeStruct((2, tracks), f32)),
        in_specs=[pl.BlockSpec(memory_space=pltpu.SMEM)] * 3 + [pl.BlockSpec(memory_space=pl.ANY)] * 4,
        out_specs=(pl.BlockSpec(memory_space=vmem),) * 2,
        scratch_shapes=[
            vmem((face_rows, tracks), f32),
            vmem((faces, block, tracks), f32),
            vmem(sub_blocks.shape, sub_blocks.dtype),
            vmem(coarse_inverse.shape, f32),
            vmem((row_blocks, block, tracks), f32),
            vmem((2, row_blocks, block, tracks), jnp.bfloat16),
            vmem((face_rows, tracks), f32),
            vmem((faces, block + n_corners, tracks), f32),
            vmem((faces, block + n_corners, tracks), f32),
            vmem((faces, block, tracks), f32),
            vmem((faces, block, tracks), f32),
            vmem((n_corners, tracks), f32),
            vmem((n_corners, tracks), f32),
            vmem((n_line, n_corners, n_plane * n_corners), f32),
            vmem((n_line, n_corners, n_plane * n_corners), f32),
            vmem((n_plane * n_corners, n_line * n_corners), f32),
            vmem((n_line, n_corners, tracks), f32),
            vmem((n_plane, n_corners, tracks), f32),
            vmem((n_plane, n_corners, tracks), f32),
            vmem((n_plane, 1, 6 * tracks), f32),
            vmem((n_line, 1, 6 * tracks), f32),
            dma((4,)),
            dma((faces,)),
            dma((faces,)),
            dma((faces,)),
            dma((faces,)),
            dma,
            dma,
            dma((5,)),
            dma((5,)),
        ],
        compiler_params=pltpu.CompilerParams(
            collective_id=0, has_side_effects=True, vmem_limit_bytes=32 * 1024 * 1024
        ),
    )(
        pattern,
        facing,
        corners,
        residual,
        direction.reshape(faces, block, tracks),
        sub_blocks,
        coarse_inverse,
    )
    residual_new = residual - factors[0:1] * image
    return residual_new, residual_new + factors[1:2] * direction


def solution(mesh):
    n_sub, n_grp, n_rep = (mesh.shape[a] for a in AXES)
    n_yl = 4 if n_sub % (4 * CORES) == 0 else 2
    sizes = (n_sub // (n_yl * CORES), n_yl, n_grp, n_rep)
    rows = P(AXES, None)
    return jax.shard_map(
        functools.partial(per_device, sizes),
        mesh=mesh,
        in_specs=(rows, rows, P(AXES, None, None, None), rows, rows, rows, rows),
        out_specs=(rows, rows),
        check_vma=False,
    )
```

time: 2430 us -> 91.6 us (0.04)
  waiting for transfers between devices: 2120 us -> 0 us
  blocking collectives: 238 us -> 0 us
  Pallas kernels: 0 us -> 83.3 us
    all_gather x1 -> x0, waiting for transfers between devices: 2110 us -> none  [per_device(): lax.all_gather(corner_totals, ('sub', 'grp', 'rep'), axis=0, tiled=True)]
    psum x2 -> x0, blocking collectives: 238 us -> none  [the longest x1 119 us: per_device(): lax.psum((local_cross, local_curve), ('sub', 'grp', 'rep'))]
    pallas_call x0 -> x1, Pallas kernels: none -> 83.3 us  [per_device(): pl.pallas_call(functools.partial(kernel, sizes), out_shape=(jax.ShapeDtyp...]
  transfers between devices with their start and end apart: 3 -> 0, of which waited for: 3 -> 0; matrix products, arithmetic and copies ran while one was open for 0% -> 0% of each run, Pallas kernels for 0% -> 0%
where the time goes in v1:
time: 91.6 us; the launch traced here: 91.3 us
  Pallas kernels  83.3 us (91%)
  local copies, waits for them, and re-layouts  6.51 us (7%)
    pallas_call x1, Pallas kernels, per_device(): pl.pallas_call(functools.partial(kernel, sizes), out_shape=(jax.ShapeDtyp...  83.3 us
    unnamed x13, local copies, waits for them, and re-layouts  6.51 us

profile of v1, /device:TPU:1, one launch (start us, length us, event | category | flops | bytes accessed | tf_op | source)
XLA Modules:
  0.0 91.3 jit_solution(3196757376041498443)
XLA Ops:
  0.6 0.8 copy.9.pattern
  1.4 0.0 copy-start
  1.4 1.6 %copy-done = bf16[16,4,128,128]{3,2,1,0:T(8,128)(2,1)S(1)} copy-done((bf16[16,4,128,128]{3,2,1,0:T(8,128)(2,1)S(1)}, bf16[16,4,128,128]{3,2,1,0:T(8,128)(2,1)}, u32[]{:S(2)}) %copy-start) | copy-done | bytes 2097176
  3.0 0.0 copy-start.1
  3.0 0.9 %copy-done.1 = f32[512,128]{1,0:T(8,128)S(1)} copy-done((f32[512,128]{1,0:T(8,128)S(1)}, f32[512,128]{1,0:T(8,128)}, u32[]{:S(2)}) %copy-start.1) | copy-done | bytes 262168
  3.9 0.0 copy-start.2
  3.9 0.9 %copy-done.2 = f32[512,128]{1,0:T(8,128)S(1)} copy-done((f32[512,128]{1,0:T(8,128)S(1)}, f32[512,128]{1,0:T(8,128)}, u32[]{:S(2)}) %copy-start.2) | copy-done | bytes 262168
  4.9 0.0 copy-start.3
  4.9 0.9 %copy-done.3 = f32[8,8192]{1,0:T(8,128)S(1)} copy-done((f32[8,8192]{1,0:T(8,128)S(1)}, f32[8,8192]{1,0:T(8,128)}, u32[]{:S(2)}) %copy-start.3) | copy-done | bytes 262168
  5.8 0.0 copy-start.4
  5.8 0.7 copy-done.4
  6.5 0.0 copy-start.5
  6.5 0.7 copy-done.5
  7.1 83.3 %shard_map.86 = (f32[512,128]{1,0:T(8,128)S(1)}, f32[2,128]{1,0:T(2,128)S(1)}) custom-call(s32[16,4]{1,0:T(8,128)S(1)} %copy.9.pattern, s32[1,4]{1,0:T(1,128)S(1)} %copy-done.4, s32[1,8]{1,0:T(1,128)S(1)} %copy-done.5, f32[512,128]{1,0:T(8,128)S(1)} %copy-done.2, f32[4,128,128]{2,1,0:T(8,128)S(1)} %bitcast.5, bf16[16,4,128,128]{3,2,1,0:T(8,128)(2,1)S(1)} %copy-done, ...), custom_call_target="tpu_custom_call" | custom-call | tf_op jit(solution)/shard_map/pallas_call | solution.py:382
  90.4 0.8 multiply_add_fusion
  (1 shorter events, 0.0 us)
Async XLA Ops:
  1.4 1.6 %copy-start = (bf16[16,4,128,128]{3,2,1,0:T(8,128)(2,1)S(1)}, bf16[16,4,128,128]{3,2,1,0:T(8,128)(2,1)}, u32[]{:S(2)}) copy-start(bf16[16,4,128,128]{3,2,1,0:T(8,128)(2,1)} %blocks_hbm.1) | copy-start | bytes 6291460
  3.0 0.9 %copy-start.1 = (f32[512,128]{1,0:T(8,128)S(1)}, f32[512,128]{1,0:T(8,128)}, u32[]{:S(2)}) copy-start(f32[512,128]{1,0:T(8,128)} %param.8) | copy-start | bytes 786436
  3.9 0.9 %copy-start.2 = (f32[512,128]{1,0:T(8,128)S(1)}, f32[512,128]{1,0:T(8,128)}, u32[]{:S(2)}) copy-start(f32[512,128]{1,0:T(8,128)} %residual_hbm.1) | copy-start | bytes 786436
  4.9 0.9 %copy-start.3 = (f32[8,8192]{1,0:T(8,128)S(1)}, f32[8,8192]{1,0:T(8,128)}, u32[]{:S(2)}) copy-start(f32[8,8192]{1,0:T(8,128)} %coarse_hbm.1) | copy-start | bytes 786436
  5.8 0.7 copy-start.4
  6.5 0.7 copy-start.5

commit v2 on v1

--- a/solution.py
+++ b/solution.py
@@ -60,15 +60,18 @@
 
 def kernel(
     sizes,
-    pattern,
-    facing,
-    corners,
+    pattern_hbm,
+    facing_hbm,
+    corners_hbm,
     residual_hbm,
     direction_hbm,
     blocks_hbm,
     coarse_hbm,
     image,
     factors,
+    pattern,
+    facing,
+    corners,
     residual,
     direction,
     blocks,
@@ -90,6 +93,7 @@
     part_in,
     sums_plane,
     sums_line,
+    sums_pair,
     load_sem,
     forward_send,
     forward_recv,
@@ -99,6 +103,8 @@
     corner_recv,
     group_send,
     group_recv,
+    pair_send,
+    pair_recv,
 ):
     n_z, n_yl, n_grp, n_rep = sizes
     n_line, n_plane = n_z * CORES, n_yl * n_grp * n_rep
@@ -112,19 +118,41 @@
     sub, grp, rep = (lax.axis_index(a) for a in AXES)
     k = (sub * n_grp + grp) * n_rep + rep
     core, yl, z = sub % CORES, (sub // CORES) % n_yl, sub // (CORES * n_yl)
-    line = z * CORES + core
+    line = core * n_z + z
     plane = (yl * n_grp + grp) * n_rep + rep
 
     def device_of(index):
         return (index // (n_grp * n_rep), (index // n_rep) % n_grp, index % n_rep)
 
+    def ring(step, size):
+        return min(step, size - step)
+
+    z_steps = sorted(range(1, n_z), key=lambda step: -ring(step, n_z))
+
+    def plane_hops(step):
+        over_y = ring(step // (n_grp * n_rep), n_yl)
+        if step % n_rep:
+            over_y = n_yl - over_y
+        return over_y + ring(step // n_rep % n_grp, n_grp)
+
+    plane_steps = sorted(range(1, n_plane), key=lambda step: -plane_hops(step))
+
+    def plane_at(step):
+        there_yl = (yl + step // (n_grp * n_rep)) % n_yl
+        there_grp = (grp + step // n_rep % n_grp) % n_grp
+        return (there_yl * n_grp + there_grp) * n_rep + (rep + step) % n_rep
+
     def on_line(place):
-        return ((place // CORES * n_yl + yl) * CORES + place % CORES, grp, rep)
+        return ((place % n_z * n_yl + yl) * CORES + place // n_z, grp, rep)
 
     def on_plane(place):
         there = (z * n_yl + place // (n_grp * n_rep)) * CORES + core
         return (there, (place // n_rep) % n_grp, place % n_rep)
 
+    def along_z(place):
+        return ((place * n_yl + yl) * CORES + core, grp, rep)
+
+    sibling = ((z * n_yl + yl) * CORES + 1 - core, grp, rep)
     above, below = device_of((k + 1) % count), device_of((k + count - 1) % count)
 
     barrier = pltpu.get_barrier_semaphore()
@@ -134,23 +162,31 @@
 
     greet(above)
     greet(below)
-
-    @pl.loop(1, n_line)
-    def _(j):
-        greet(on_line((line + j) % n_line))
-
-    @pl.loop(1, n_plane)
-    def _(j):
-        greet(on_plane((plane + j) % n_plane))
+    for step in z_steps:
+        for other in range(CORES):
+            greet((((z + step) % n_z * n_yl + yl) * CORES + other, grp, rep))
+    for step in plane_steps:
+        greet(on_plane(plane_at(step)))
+    greet(sibling)
 
     loads = [
         pltpu.make_async_copy(a, b, load_sem.at[i])
         for i, (a, b) in enumerate(
-            ((direction_hbm, direction), (coarse_hbm, coarse), (residual_hbm, residual), (blocks_hbm, blocks))
+            (
+                (facing_hbm, facing),
+                (corners_hbm, corners),
+                (direction_hbm, direction),
+                (coarse_hbm, coarse),
+                (residual_hbm, residual),
+                (pattern_hbm, pattern),
+                (blocks_hbm, blocks),
+            )
         )
     ]
     for load in loads:
         load.start()
+    for load in loads[:3]:
+        load.wait()
 
     back_at = []
     for v in range(faces):
@@ -159,7 +195,6 @@
             place = jnp.where(facing[0, b] == v, b, place)
         back_at.append(place)
 
-    loads[0].wait()
     for b in range(faces):
         forward_out[b, :block] = direction[facing[0, b]]
     rows8 = lax.broadcasted_iota(jnp.int32, (n_corners, tracks), 0)
@@ -168,7 +203,7 @@
         wanted = jnp.where(rows8 == i, back_at[i // per_block] * block + corners[0, i] % block, wanted)
     forward_out[faces - 1, block:] = wanted.astype(jnp.float32)
 
-    loads[1].wait()
+    loads[3].wait()
     lanes = lax.broadcasted_iota(jnp.int32, (n_corners, LANES), 1)
     half = LANES // CORES
     for zz in range(n_z):
@@ -176,8 +211,8 @@
             first = coarse[:, pl.ds((zz * n_yl + 2 * q) * LANES, LANES)]
             second = coarse[:, pl.ds((zz * n_yl + 2 * q + 1) * LANES, LANES)]
             at = pl.ds(q * LANES, LANES)
-            packed[zz * CORES, :, at] = jnp.where(lanes < half, first, pltpu.roll(second, half, 1))
-            packed[zz * CORES + 1, :, at] = jnp.where(lanes < half, pltpu.roll(first, half, 1), second)
+            packed[zz, :, at] = jnp.where(lanes < half, first, pltpu.roll(second, half, 1))
+            packed[n_z + zz, :, at] = jnp.where(lanes < half, pltpu.roll(first, half, 1), second)
 
     pl.semaphore_wait(barrier, n_line + n_plane)
 
@@ -207,6 +242,18 @@
                 source_of(there), target.at[mine], group_send.at[stage], group_recv.at[stage], where(there)
             ).start()
 
+    def send_all(stage, places, where, mine, source_of, target):
+        for there in places:
+            remote(
+                source_of(there), target.at[mine], group_send.at[stage], group_recv.at[stage], where(there)
+            ).start()
+
+    def over_z(stage, source_of, target):
+        send_all(stage, [(z + step) % n_z for step in z_steps], along_z, z, source_of, target)
+
+    def over_plane(stage, source_of, target):
+        send_all(stage, [plane_at(step) for step in plane_steps], on_plane, plane, source_of, target)
+
     def all_of(stage, size, target, sems):
         rest = target.at[pl.ds(0, size - 1)]
         return pltpu.make_async_copy(rest, rest, sems.at[stage])
@@ -216,7 +263,7 @@
 
     rows32 = 32
     zero = (jnp.zeros((rows32, tracks), jnp.float32),) * 2
-    loads[2].wait()
+    loads[4].wait()
 
     def add_old(i, total):
         r = residual[pl.ds(pl.multiple_of(i * rows32, rows32), rows32)]
@@ -229,7 +276,8 @@
     for b in range(faces):
         source[faces + b] = direction[b]
         rounded[0, faces + b] = direction[b].astype(rounded.dtype)
-    loads[3].wait()
+    loads[5].wait()
+    loads[6].wait()
     for b in range(faces):
         forward[b].wait_recv()
     for b in range(faces):
@@ -237,25 +285,27 @@
         source[b] = arrived
         rounded[0, b] = arrived.astype(rounded.dtype)
 
-    def relaxed(r, now):
-        left = jnp.concatenate([blocks[r, j] for j in range(nnz)], axis=1)
-        right = jnp.concatenate([rounded[now, pattern[r, j]] for j in range(nnz)], axis=0)
-        return source[r] - jnp.dot(left, right, preferred_element_type=jnp.float32)
+    def relaxed(pair, now):
+        rows = (2 * pair, 2 * pair + 1)
+        left = [jnp.concatenate([blocks[r, j] for j in range(nnz)], axis=1) for r in rows]
+        right = [jnp.concatenate([rounded[now, pattern[j, r]] for j in range(nnz)], axis=0) for r in rows]
+        product = jnp.dot(
+            jnp.concatenate(left, axis=0), jnp.concatenate(right, axis=1), preferred_element_type=jnp.float32
+        )
+        return source[rows[0]] - product[:block, :tracks], source[rows[1]] - product[block:, tracks:]
 
     for sweep in range(SWEEPS - 1):
 
-        def step(r, carry, now=sweep % 2):
-            rounded[1 - now, r] = relaxed(r, now).astype(rounded.dtype)
+        def step(pair, carry, now=sweep % 2):
+            first, second = relaxed(pair, now)
+            rounded[1 - now, 2 * pair] = first.astype(rounded.dtype)
+            rounded[1 - now, 2 * pair + 1] = second.astype(rounded.dtype)
             return carry
 
-        lax.fori_loop(0, row_blocks, step, 0, unroll=4)
+        lax.fori_loop(0, row_blocks // 2, step, 0, unroll=2)
     last = (SWEEPS - 1) % 2
-
-    def step_lower(r, carry):
-        back_out[r] = relaxed(r, last)
-        return carry
-
-    lax.fori_loop(0, faces, step_lower, 0, unroll=True)
+    for pair in range(faces // 2):
+        back_out[2 * pair], back_out[2 * pair + 1] = relaxed(pair, last)
 
     rows_seg = lax.broadcasted_iota(jnp.int32, (segment, tracks), 0)
     found = jnp.zeros((n_corners, tracks), jnp.float32)
@@ -277,11 +327,9 @@
     for copy in back:
         copy.start()
 
-    def step_upper(r, carry):
-        upper[pl.ds(pl.multiple_of((r - faces) * block, block), block)] = relaxed(r, last)
-        return carry
-
-    lax.fori_loop(faces, 2 * faces, step_upper, 0, unroll=True)
+    for pair in range(faces // 2):
+        start = 2 * pair * block
+        upper[start : start + block], upper[start + block : start + 2 * block] = relaxed(faces // 2 + pair, last)
     own = jnp.zeros((n_corners, tracks), jnp.float32)
     for i in range(n_corners):
         own = jnp.where(rows8 == i, upper[pl.ds(corners[0, i], 1)], own)
@@ -291,21 +339,24 @@
 
     corner_copy.wait_recv()
     at_corners = jnp.where(k < count - 1, corner_in[...], 0.0)
-    totals[line] = own + at_corners
-    exchange(1, n_line, line, on_line, lambda there: totals.at[line], totals)
+    totals[core, z] = own + at_corners
+    over_z(1, lambda there: totals.at[core, z], totals.at[core])
     own_jump = own - at_corners
     own_residual = jnp.zeros((n_corners, tracks), jnp.float32)
     for i in range(n_corners):
         own_residual = jnp.where(rows8 == i, residual[pl.ds(corners[0, i], 1)], own_residual)
 
-    all_of(1, n_line, totals, group_recv).wait()
+    all_of(1, n_z, totals.at[core], group_recv).wait()
+    to_sibling = remote(totals.at[core], totals.at[core], pair_send.at[0], pair_recv.at[0], sibling)
+    to_sibling.start()
+    to_sibling.wait_recv()
     part[...] = jnp.dot(
         turned[...],
         totals[...].reshape(n_line * n_corners, tracks),
         precision=lax.Precision.HIGHEST,
         preferred_element_type=jnp.float32,
     ).reshape(n_plane, n_corners, tracks)
-    exchange(2, n_plane, plane, on_plane, lambda there: part.at[there], part_in)
+    over_plane(2, lambda there: part.at[there], part_in)
     part_in[plane] = part[plane]
 
     for copy in back:
@@ -333,7 +384,7 @@
 
     mine = jnp.concatenate([old[0], cross[0], curve[0], old[1], cross[1], curve[1]], axis=1)
     sums_plane[plane] = mine
-    exchange(3, n_plane, plane, on_plane, lambda there: sums_plane.at[plane], sums_plane)
+    over_plane(3, lambda there: sums_plane.at[plane], sums_plane)
     for i in range(n_corners):
         for piece in range(segment // rows32):
             start = i * segment + piece * rows32
@@ -345,10 +396,14 @@
         return tuple(v.reshape(1, 3 * tracks) for v in tidy(pair))
 
     all_of(3, n_plane, sums_plane, group_recv).wait()
-    sums_line[line] = jnp.concatenate(total_of(sums_plane), axis=1)
-    exchange(4, n_line, line, on_line, lambda there: sums_line.at[line], sums_line)
-    all_of(4, n_line, sums_line, group_recv).wait()
-    pair = total_of(sums_line)
+    sums_line[z] = jnp.concatenate(total_of(sums_plane), axis=1)
+    over_z(4, lambda there: sums_line.at[z], sums_line)
+    all_of(4, n_z, sums_line, group_recv).wait()
+    sums_pair[core] = jnp.concatenate(total_of(sums_line), axis=1)
+    sums_to_sibling = remote(sums_pair.at[core], sums_pair.at[core], pair_send.at[1], pair_recv.at[1], sibling)
+    sums_to_sibling.start()
+    sums_to_sibling.wait_recv()
+    pair = total_of(sums_pair)
     old, cross, curve = (
         tuple(v[:, i * tracks : (i + 1) * tracks] for v in pair) for i in range(3)
     )
@@ -362,11 +417,10 @@
     factors[0:1] = length
     factors[1:2] = jnp.maximum(new[0], 0.0) / old[0]
 
-    for copy in forward + back:
+    for copy in forward + back + [corner_copy, to_sibling, sums_to_sibling]:
         copy.wait_send()
-    corner_copy.wait_send()
     for stage, (size, buffer) in enumerate(
-        ((n_line, columns), (n_line, totals), (n_plane, part_in), (n_plane, sums_plane), (n_line, sums_line))
+        ((n_line, columns), (n_z, totals.at[0]), (n_plane, part_in), (n_plane, sums_plane), (n_z, sums_line))
     ):
         all_of(stage, size, buffer, group_send).wait()
 
@@ -377,14 +431,17 @@
     face_rows, tracks = residual.shape
     row_blocks, nnz, block, _ = sub_blocks.shape
     faces, n_corners = facing.shape[1], corners.shape[1]
-    f32, vmem = jnp.float32, pltpu.VMEM
+    f32, vmem, smem = jnp.float32, pltpu.VMEM, pltpu.SMEM
     dma = pltpu.SemaphoreType.DMA
     image, factors = pl.pallas_call(
         functools.partial(kernel, sizes),
         out_shape=(jax.ShapeDtypeStruct((face_rows, tracks), f32), jax.ShapeDtypeStruct((2, tracks), f32)),
-        in_specs=[pl.BlockSpec(memory_space=pltpu.SMEM)] * 3 + [pl.BlockSpec(memory_space=pl.ANY)] * 4,
+        in_specs=[pl.BlockSpec(memory_space=pltpu.HBM)] * 7,
         out_specs=(pl.BlockSpec(memory_space=vmem),) * 2,
         scratch_shapes=[
+            smem((nnz, row_blocks), jnp.int32),
+            smem(facing.shape, jnp.int32),
+            smem(corners.shape, jnp.int32),
             vmem((face_rows, tracks), f32),
             vmem((faces, block, tracks), f32),
             vmem(sub_blocks.shape, sub_blocks.dtype),
@@ -401,12 +458,13 @@
             vmem((n_line, n_corners, n_plane * n_corners), f32),
             vmem((n_line, n_corners, n_plane * n_corners), f32),
             vmem((n_plane * n_corners, n_line * n_corners), f32),
-            vmem((n_line, n_corners, tracks), f32),
+            vmem((CORES, n_z, n_corners, tracks), f32),
             vmem((n_plane, n_corners, tracks), f32),
             vmem((n_plane, n_corners, tracks), f32),
             vmem((n_plane, 1, 6 * tracks), f32),
-            vmem((n_line, 1, 6 * tracks), f32),
-            dma((4,)),
+            vmem((n_z, 1, 6 * tracks), f32),
+            vmem((CORES, 1, 6 * tracks), f32),
+            dma((7,)),
             dma((faces,)),
             dma((faces,)),
             dma((faces,)),
@@ -415,12 +473,14 @@
             dma,
             dma((5,)),
             dma((5,)),
+            dma((2,)),
+            dma((2,)),
         ],
         compiler_params=pltpu.CompilerParams(
-            collective_id=0, has_side_effects=True, vmem_limit_bytes=32 * 1024 * 1024
+            collective_id=0, has_side_effects=True, vmem_limit_bytes=62 * 1024 * 1024
         ),
     )(
-        pattern,
+        pattern.T,
         facing,
         corners,
         residual,

time: 91.6 us -> 85.2 us (0.930)
  local copies, waits for them, and re-layouts: 6.51 us -> 0.77 us
  Pallas kernels: 83.3 us -> 81.8 us
  other arithmetic: 0.84 us -> 1.78 us
    unnamed x13 -> x4, local copies, waits for them, and re-layouts: 6.51 us -> 0.01 us
    pallas_call x1, Pallas kernels: 83.3 us -> 81.8 us  [per_device(): pl.pallas_call(functools.partial(kernel, sizes), out_shape=(jax.ShapeDtyp...]
    add x1, other arithmetic: 0.84 us -> 1.78 us  [per_device(): return (residual_new, residual_new + factors[1:2] * direction)]
where the time goes in v2:
time: 85.2 us; the launch traced here: 85 us
  Pallas kernels  81.8 us (96%)
  other arithmetic  1.78 us (2%)
    pallas_call x1, Pallas kernels, per_device(): pl.pallas_call(functools.partial(kernel, sizes), out_shape=(jax.ShapeDtyp...  81.8 us
    add x1, other arithmetic, per_device(): return (residual_new, residual_new + factors[1:2] * direction)  1.78 us

profile of v2, /device:TPU:1, one launch (start us, length us, event | category | flops | bytes accessed | tf_op | source)
XLA Modules:
  0.0 85.0 jit_solution(7343911002534539083)
XLA Ops:
  0.6 0.0 copy-start
  0.6 0.0 copy-start.1
  0.7 81.8 %shard_map.86 = (f32[512,128]{1,0:T(8,128)}, f32[2,128]{1,0:T(2,128)}) custom-call(s32[4,16]{1,0:T(4,128)} %bitcast.7, s32[1,4]{1,0:T(1,128)} %facing_hbm.1, s32[1,8]{1,0:T(1,128)} %corners_hbm.1, f32[512,128]{1,0:T(8,128)} %residual_hbm.1, f32[4,128,128]{2,1,0:T(8,128)} %bitcast.6, bf16[16,4,128,128]{3,2,1,0:T(8,128)(2,1)} %blocks_hbm.1, f32[8,8192]{1,0:T(8,128)} %coarse_hbm.1), custom_call_target="tpu_custom_call" | custom-call | tf_op jit(solution)/shard_map/pallas_call | solution.py:436
  82.5 0.8 slice_bitcast_fusion.1
  83.3 0.0 copy-done
  83.3 0.0 copy-done.1
  83.3 1.8 %multiply_add_fusion = (f32[512,128]{1,0:T(8,128)}, f32[512,128]{1,0:T(8,128)}) fusion(f32[512,128]{1,0:T(8,128)S(1)} %copy-done, f32[128]{0:T(128)S(1)} %get-tuple-element.9, f32[512,128]{1,0:T(8,128)S(1)} %copy-done.1, f32[512,128]{1,0:T(8,128)} %get-tuple-element.5, f32[128]{0:T(128)S(1)} %get-tuple-element.8), kind=kLoop, calls=%fused_computation | loop fusion | flops 262144 | bytes 1311744 | tf_op jit(solution)/shard_map/add | solution.py:492
Async XLA Ops:
  0.6 82.6 %copy-start = (f32[512,128]{1,0:T(8,128)S(1)}, f32[512,128]{1,0:T(8,128)}, u32[]{:S(2)}) copy-start(f32[512,128]{1,0:T(8,128)} %param.8) | copy-start | bytes 786436
  0.6 82.6 %copy-start.1 = (f32[512,128]{1,0:T(8,128)S(1)}, f32[512,128]{1,0:T(8,128)}, u32[]{:S(2)}) copy-start(f32[512,128]{1,0:T(8,128)} %residual_hbm.1) | copy-start | bytes 786436

commit v3 on v2

--- a/solution.py
+++ b/solution.py
@@ -67,17 +67,19 @@
     direction_hbm,
     blocks_hbm,
     coarse_hbm,
-    image,
+    image_hbm,
     factors,
     pattern,
     facing,
     corners,
+    image,
     residual,
     direction,
     blocks,
     coarse,
     source,
     rounded,
+    rounded_next,
     upper,
     forward_out,
     forward_in,
@@ -272,40 +274,38 @@
     old = fold(lax.fori_loop(0, faces * block // rows32, add_old, zero))
     for r in range(2 * faces, row_blocks):
         source[r] = jnp.zeros((block, tracks), jnp.float32)
-        rounded[0, r] = jnp.zeros((block, tracks), rounded.dtype)
+        rounded[r] = jnp.zeros((block, tracks), rounded.dtype)
     for b in range(faces):
         source[faces + b] = direction[b]
-        rounded[0, faces + b] = direction[b].astype(rounded.dtype)
+        rounded[faces + b] = direction[b].astype(rounded.dtype)
     loads[5].wait()
     loads[6].wait()
     for b in range(faces):
         forward[b].wait_recv()
-    for b in range(faces):
         arrived = jnp.where(k > 0, -forward_in[b, :block], 0.0)
         source[b] = arrived
-        rounded[0, b] = arrived.astype(rounded.dtype)
-
-    def relaxed(pair, now):
-        rows = (2 * pair, 2 * pair + 1)
-        left = [jnp.concatenate([blocks[r, j] for j in range(nnz)], axis=1) for r in rows]
-        right = [jnp.concatenate([rounded[now, pattern[j, r]] for j in range(nnz)], axis=0) for r in rows]
-        product = jnp.dot(
-            jnp.concatenate(left, axis=0), jnp.concatenate(right, axis=1), preferred_element_type=jnp.float32
-        )
-        return source[rows[0]] - product[:block, :tracks], source[rows[1]] - product[block:, tracks:]
-
-    for sweep in range(SWEEPS - 1):
-
-        def step(pair, carry, now=sweep % 2):
-            first, second = relaxed(pair, now)
-            rounded[1 - now, 2 * pair] = first.astype(rounded.dtype)
-            rounded[1 - now, 2 * pair + 1] = second.astype(rounded.dtype)
+        rounded[b] = arrived.astype(rounded.dtype)
+
+    def relaxed(r, now):
+        left = jnp.concatenate([blocks[r, j] for j in range(nnz)], axis=1)
+        right = jnp.concatenate([now[pattern[j, r]] for j in range(nnz)], axis=0)
+        return source[r] - jnp.dot(left, right, preferred_element_type=jnp.float32)
+
+    now, later = rounded, rounded_next
+    for _ in range(SWEEPS - 1):
+
+        def step(r, carry, now=now, later=later):
+            later[r] = relaxed(r, now).astype(later.dtype)
             return carry
 
-        lax.fori_loop(0, row_blocks // 2, step, 0, unroll=2)
-    last = (SWEEPS - 1) % 2
-    for pair in range(faces // 2):
-        back_out[2 * pair], back_out[2 * pair + 1] = relaxed(pair, last)
+        lax.fori_loop(0, row_blocks, step, 0, unroll=True)
+        now, later = later, now
+
+    def step_lower(r, carry, now=now):
+        back_out[r] = relaxed(r, now)
+        return carry
+
+    lax.fori_loop(0, faces, step_lower, 0, unroll=True)
 
     rows_seg = lax.broadcasted_iota(jnp.int32, (segment, tracks), 0)
     found = jnp.zeros((n_corners, tracks), jnp.float32)
@@ -324,12 +324,13 @@
     back = [
         remote(back_out.at[b], back_in.at[b], back_send.at[b], back_recv.at[b], below) for b in range(faces)
     ]
-    for copy in back:
-        copy.start()
-
-    for pair in range(faces // 2):
-        start = 2 * pair * block
-        upper[start : start + block], upper[start + block : start + 2 * block] = relaxed(faces // 2 + pair, last)
+
+
+    def step_upper(r, carry, now=now):
+        upper[pl.ds(pl.multiple_of(r * block, block), block)] = relaxed(faces + r, now)
+        return carry
+
+    lax.fori_loop(0, faces, step_upper, 0, unroll=True)
     own = jnp.zeros((n_corners, tracks), jnp.float32)
     for i in range(n_corners):
         own = jnp.where(rows8 == i, upper[pl.ds(corners[0, i], 1)], own)
@@ -341,6 +342,8 @@
     at_corners = jnp.where(k < count - 1, corner_in[...], 0.0)
     totals[core, z] = own + at_corners
     over_z(1, lambda there: totals.at[core, z], totals.at[core])
+    for copy in back:
+        copy.start()
     own_jump = own - at_corners
     own_residual = jnp.zeros((n_corners, tracks), jnp.float32)
     for i in range(n_corners):
@@ -390,6 +393,9 @@
             start = i * segment + piece * rows32
             added = jnp.where(rows_in + start == corners[0, i], coarse_part[i : i + 1], 0.0)
             image[start : start + rows32] = image[start : start + rows32] + added
+
+    store = pltpu.make_async_copy(image, image_hbm, load_sem.at[0])
+    store.start()
 
     def total_of(buffer):
         pair = fold((buffer[:, :, : 3 * tracks], buffer[:, :, 3 * tracks :]))
@@ -417,6 +423,7 @@
     factors[0:1] = length
     factors[1:2] = jnp.maximum(new[0], 0.0) / old[0]
 
+    store.wait()
     for copy in forward + back + [corner_copy, to_sibling, sums_to_sibling]:
         copy.wait_send()
     for stage, (size, buffer) in enumerate(
@@ -437,17 +444,19 @@
         functools.partial(kernel, sizes),
         out_shape=(jax.ShapeDtypeStruct((face_rows, tracks), f32), jax.ShapeDtypeStruct((2, tracks), f32)),
         in_specs=[pl.BlockSpec(memory_space=pltpu.HBM)] * 7,
-        out_specs=(pl.BlockSpec(memory_space=vmem),) * 2,
+        out_specs=(pl.BlockSpec(memory_space=pl.ANY), pl.BlockSpec(memory_space=vmem)),
         scratch_shapes=[
             smem((nnz, row_blocks), jnp.int32),
             smem(facing.shape, jnp.int32),
             smem(corners.shape, jnp.int32),
             vmem((face_rows, tracks), f32),
+            vmem((face_rows, tracks), f32),
             vmem((faces, block, tracks), f32),
             vmem(sub_blocks.shape, sub_blocks.dtype),
             vmem(coarse_inverse.shape, f32),
             vmem((row_blocks, block, tracks), f32),
-            vmem((2, row_blocks, block, tracks), jnp.bfloat16),
+            vmem((row_blocks, block, tracks), jnp.bfloat16),
+            vmem((row_blocks, block, tracks), jnp.bfloat16),
             vmem((face_rows, tracks), f32),
             vmem((faces, block + n_corners, tracks), f32),
             vmem((faces, block + n_corners, tracks), f32),

time: 85.2 us -> 82.2 us (0.965)
  Pallas kernels: 81.8 us -> 78.8 us
    pallas_call x1, Pallas kernels: 81.8 us -> 78.8 us  [per_device(): pl.pallas_call(functools.partial(kernel, sizes), out_shape=(jax.ShapeDtyp...]
where the time goes in v3:
time: 82.2 us; the launch traced here: 82 us
  Pallas kernels  78.8 us (96%)
  other arithmetic  1.78 us (2%)
    pallas_call x1, Pallas kernels, per_device(): pl.pallas_call(functools.partial(kernel, sizes), out_shape=(jax.ShapeDtyp...  78.8 us
    add x1, other arithmetic, per_device(): return (residual_new, residual_new + factors[1:2] * direction)  1.78 us

profile of v3, /device:TPU:1, one launch (start us, length us, event | category | flops | bytes accessed | tf_op | source)
XLA Modules:
  0.0 82.0 jit_solution(5218981534212946663)
XLA Ops:
  0.6 0.0 copy-start
  0.6 0.0 copy-start.1
  0.7 78.8 %shard_map.86 = (f32[512,128]{1,0:T(8,128)}, f32[2,128]{1,0:T(2,128)}) custom-call(s32[4,16]{1,0:T(4,128)} %bitcast.7, s32[1,4]{1,0:T(1,128)} %facing_hbm.1, s32[1,8]{1,0:T(1,128)} %corners_hbm.1, f32[512,128]{1,0:T(8,128)} %residual_hbm.1, f32[4,128,128]{2,1,0:T(8,128)} %bitcast.6, bf16[16,4,128,128]{3,2,1,0:T(8,128)(2,1)} %blocks_hbm.1, f32[8,8192]{1,0:T(8,128)} %coarse_hbm.1), custom_call_target="tpu_custom_call" | custom-call | tf_op jit(solution)/shard_map/pallas_call | solution.py:443
  79.4 0.8 slice_bitcast_fusion.1
  80.2 0.0 copy-done
  80.2 0.0 copy-done.1
  80.2 1.8 %multiply_add_fusion = (f32[512,128]{1,0:T(8,128)}, f32[512,128]{1,0:T(8,128)}) fusion(f32[512,128]{1,0:T(8,128)S(1)} %copy-done, f32[128]{0:T(128)S(1)} %get-tuple-element.9, f32[512,128]{1,0:T(8,128)S(1)} %copy-done.1, f32[512,128]{1,0:T(8,128)} %get-tuple-element.5, f32[128]{0:T(128)S(1)} %get-tuple-element.8), kind=kLoop, calls=%fused_computation | loop fusion | flops 262144 | bytes 1311744 | tf_op jit(solution)/shard_map/add | solution.py:501
Async XLA Ops:
  0.6 79.6 %copy-start = (f32[512,128]{1,0:T(8,128)S(1)}, f32[512,128]{1,0:T(8,128)}, u32[]{:S(2)}) copy-start(f32[512,128]{1,0:T(8,128)} %param.8) | copy-start | bytes 786436
  0.6 79.6 %copy-start.1 = (f32[512,128]{1,0:T(8,128)S(1)}, f32[512,128]{1,0:T(8,128)}, u32[]{:S(2)}) copy-start(f32[512,128]{1,0:T(8,128)} %residual_hbm.1) | copy-start | bytes 786436

commit v4 on v3

--- a/solution.py
+++ b/solution.py
@@ -335,8 +335,6 @@
     for i in range(n_corners):
         own = jnp.where(rows8 == i, upper[pl.ds(corners[0, i], 1)], own)
 
-    all_of(0, n_line, columns, group_recv).wait()
-    turned[...] = columns[...].reshape(n_line * n_corners, n_plane * n_corners).T
 
     corner_copy.wait_recv()
     at_corners = jnp.where(k < count - 1, corner_in[...], 0.0)
@@ -349,6 +347,8 @@
     for i in range(n_corners):
         own_residual = jnp.where(rows8 == i, residual[pl.ds(corners[0, i], 1)], own_residual)
 
+    all_of(0, n_line, columns, group_recv).wait()
+    turned[...] = columns[...].reshape(n_line * n_corners, n_plane * n_corners).T
     all_of(1, n_z, totals.at[core], group_recv).wait()
     to_sibling = remote(totals.at[core], totals.at[core], pair_send.at[0], pair_recv.at[0], sibling)
     to_sibling.start()

time: 82.2 us -> 82.2 us (level)
  no operation moved by 1% of the time
where the time goes in v4:
time: 82.2 us; the launch traced here: 82 us
  Pallas kernels  78.8 us (96%)
  other arithmetic  1.78 us (2%)
    pallas_call x1, Pallas kernels, per_device(): pl.pallas_call(functools.partial(kernel, sizes), out_shape=(jax.ShapeDtyp...  78.8 us
    add x1, other arithmetic, per_device(): return (residual_new, residual_new + factors[1:2] * direction)  1.78 us

profile of v4, /device:TPU:1, one launch (start us, length us, event | category | flops | bytes accessed | tf_op | source)
XLA Modules:
  0.0 82.0 jit_solution(7346201443372406053)
XLA Ops:
  0.6 0.0 copy-start
  0.6 0.0 copy-start.1
  0.7 78.8 %shard_map.86 = (f32[512,128]{1,0:T(8,128)}, f32[2,128]{1,0:T(2,128)}) custom-call(s32[4,16]{1,0:T(4,128)} %bitcast.7, s32[1,4]{1,0:T(1,128)} %facing_hbm.1, s32[1,8]{1,0:T(1,128)} %corners_hbm.1, f32[512,128]{1,0:T(8,128)} %residual_hbm.1, f32[4,128,128]{2,1,0:T(8,128)} %bitcast.6, bf16[16,4,128,128]{3,2,1,0:T(8,128)(2,1)} %blocks_hbm.1, f32[8,8192]{1,0:T(8,128)} %coarse_hbm.1), custom_call_target="tpu_custom_call" | custom-call | tf_op jit(solution)/shard_map/pallas_call | solution.py:443
  79.4 0.8 slice_bitcast_fusion.1
  80.2 0.0 copy-done
  80.2 0.0 copy-done.1
  80.2 1.8 %multiply_add_fusion = (f32[512,128]{1,0:T(8,128)}, f32[512,128]{1,0:T(8,128)}) fusion(f32[512,128]{1,0:T(8,128)S(1)} %copy-done, f32[128]{0:T(128)S(1)} %get-tuple-element.9, f32[512,128]{1,0:T(8,128)S(1)} %copy-done.1, f32[512,128]{1,0:T(8,128)} %get-tuple-element.5, f32[128]{0:T(128)S(1)} %get-tuple-element.8), kind=kLoop, calls=%fused_computation | loop fusion | flops 262144 | bytes 1311744 | tf_op jit(solution)/shard_map/add | solution.py:501
Async XLA Ops:
  0.6 79.5 %copy-start = (f32[512,128]{1,0:T(8,128)S(1)}, f32[512,128]{1,0:T(8,128)}, u32[]{:S(2)}) copy-start(f32[512,128]{1,0:T(8,128)} %param.8) | copy-start | bytes 786436
  0.6 79.5 %copy-start.1 = (f32[512,128]{1,0:T(8,128)S(1)}, f32[512,128]{1,0:T(8,128)}, u32[]{:S(2)}) copy-start(f32[512,128]{1,0:T(8,128)} %residual_hbm.1) | copy-start | bytes 786436
